TPU v7x, 32 devices: a whole 2x2x4 slice. The times are simulated.
32 devices in a mesh: groups: 2 (over x), pool: 8 (over z, y), tensor: 2 (over core).
Axes of the slice: x: 2, y: 2, z: 4, core: 2. Of those that a mesh axis runs over, the one named last changes fastest.
Arguments:
- hidden: bfloat16 [384, 8192], P(('groups', 'pool'), 'tensor'), parts along dimension 0, may hold values from -6 to 6
- adapter_ids: int32 [384, 1], P(('groups', 'pool')), parts along dimension 0, may hold values from 0 to 7; in each aligned block of 24 rows (0 to 23, 24 to 47, ...) at most 6 rows name the same one
- page_table: int32 [8], replicated, may hold values from 0 to 7, each once
- gate_weight: bfloat16 [8192, 14336], P('tensor', 'pool'), may hold values from -0.0625 to 0.0625
- up_weight: bfloat16 [8192, 14336], P('tensor', 'pool'), may hold values from -0.0625 to 0.0625
- shrink: bfloat16 [8, 8192, 64], P('pool', 'tensor'), may hold values from -0.0625 to 0.0625
- gate_expander_matrices: bfloat16 [8, 32, 14336], P(None, None, 'pool'), may hold values from -1 to 1
- up_expander_matrices: bfloat16 [8, 32, 14336], P(None, None, 'pool'), may hold values from -1 to 1
Outputs:
- activated: bfloat16 [384, 14336], P(('groups', 'pool')), parts along dimension 0
There are 2 independent parts, one for each index of `groups`. A program takes and returns all parts, laid end to end along the dimension named above; an argument that names none is the same for every part. Nothing has to cross between parts.
Inputs may be any that keep to these rules, and one draw needn't show every extreme that they name: `adapter_ids`: in the 24 rows of one pool device no adapter is named by more than 6 rows, and in some device's rows one adapter is named by exactly 6; every adapter is named by some row. `page_table`: each slot is held by exactly one adapter.
All inputs are finite; a program needn't handle non-finite values.
Results may differ from a plain program's by a relative error of at most 0.0037.
Values may be sent and summed in bfloat16 or wider, within the bound.
A program may use at most 128 MiB of HBM per device.

v0:
```python
import jax
import jax.numpy as jnp
from jax import lax
from jax.sharding import PartitionSpec as P

adapter_scale_factor = 0.5


def expansion_products(shrunk_part, hot_part, gate_expander_matrices, up_expander_matrices):
    rank = gate_expander_matrices.shape[1]
    number = hot_part.shape[0]
    width = gate_expander_matrices.shape[2]
    gate_in = (hot_part[:, :, None] * shrunk_part[:, None, :rank]).reshape(number, -1)
    up_in = (hot_part[:, :, None] * shrunk_part[:, None, rank:]).reshape(number, -1)
    gate_adapter_change = jnp.dot(
        gate_in, gate_expander_matrices.reshape(-1, width), preferred_element_type=jnp.float32
    )
    up_adapter_change = jnp.dot(
        up_in, up_expander_matrices.reshape(-1, width), preferred_element_type=jnp.float32
    )
    return jnp.concatenate([gate_adapter_change, up_adapter_change], axis=1)


def body(
    hidden,
    adapter_ids,
    page_table,
    gate_weight,
    up_weight,
    shrink,
    gate_expander_matrices,
    up_expander_matrices,
):
    adapters = page_table.shape[0]
    columns = gate_weight.shape[1]
    table = jnp.arange(adapters, dtype=jnp.int32)
    id_hot = adapter_ids == table[None, :]
    slot = jnp.sum(jnp.where(id_hot, page_table[None, :], 0), axis=1)
    slot_hot = (slot[:, None] == table[None, :]).astype(jnp.bfloat16)
    hot_piece = slot_hot.astype(jnp.float32)
    per_slot = jnp.einsum(
        "rd,sdk->rsk",
        hidden,
        lax.all_gather(shrink, "pool", axis=0, tiled=True),
        preferred_element_type=jnp.float32,
    )
    partial_value = jnp.einsum("rsk,rs->rk", per_slot, hot_piece, precision=lax.Precision.HIGHEST)
    shrunk = lax.psum(partial_value, "tensor").astype(jnp.bfloat16)
    piece = lax.all_gather(hidden, "pool", axis=0, tiled=True)
    gate_part = jnp.dot(piece, gate_weight, preferred_element_type=jnp.float32)
    up_part = jnp.dot(piece, up_weight, preferred_element_type=jnp.float32)
    base_part = jnp.concatenate([gate_part, up_part], axis=1)
    reduced_rows_gathered = lax.all_gather(shrunk, "pool", axis=0, tiled=True)
    slot_all = lax.all_gather(slot, "pool", axis=0, tiled=True)
    active_rows_gathered = (slot_all[:, None] == table[None, :]).astype(jnp.bfloat16)
    combined_sum = lax.psum(base_part, "tensor")
    combined_sum = combined_sum + adapter_scale_factor * expansion_products(
        reduced_rows_gathered, active_rows_gathered, gate_expander_matrices, up_expander_matrices
    )
    gate_preactivation = combined_sum[:, :columns]
    up_preactivation = combined_sum[:, columns:]
    activated = (jax.nn.silu(gate_preactivation) * up_preactivation).astype(jnp.bfloat16)
    return lax.all_to_all(activated, "pool", split_axis=0, concat_axis=1, tiled=True)


def solution(mesh):
    in_specs = (
        P(("groups", "pool"), "tensor"),
        P(("groups", "pool"), None),
        P(),
        P("tensor", "pool"),
        P("tensor", "pool"),
        P("pool", "tensor", None),
        P(None, None, "pool"),
        P(None, None, "pool"),
    )
    out_specs = P(("groups", "pool"), None)
    return jax.shard_map(body, mesh=mesh, in_specs=in_specs, out_specs=out_specs, check_vma=False)
```

profile of v0, /device:TPU:0, one launch (start us, length us, event | category | flops | bytes accessed | tf_op | source)
XLA Modules:
  0.0 197.5 jit_solution(5765895506717737916)
XLA Ops:
  6.5 0.0 copy-start
  6.5 0.0 all-gather.3.cloned.1.call-start
  6.5 0.7 all-gather.3.cloned.1.call-update
  7.3 0.0 all-gather.5.cloned.1.call-start
  7.3 0.7 all-gather.5.cloned.1.call-update
  8.0 0.0 all-reduce.3.cloned.1.call-start
  8.1 48.4 %all-gather.3.cloned.1.call-done = bf16[192,4096]{1,0:T(8,128)(2,1)} async-done(((bf16[24,4096]{1,0:T(8,128)(2,1)}), bf16[192,4096]{1,0:T(8,128)(2,1)}) %all-gather.3.cloned.1.call-update) | async-done | bytes 1572880 | tf_op jit(solution)/shard_map/all_gather | solution.py:49
  56.5 0.0 copy-start.2
  56.5 9.2 %fusion.17 = f32[192,1792]{1,0:T(8,128)S(1)} fusion(bf16[192,4096]{1,0:T(8,128)(2,1)} %all-gather.3.cloned.1.call-done, bf16[4096,1792]{1,0:T(8,128)(2,1)} %param.12), kind=kOutput, calls=%fused_computation.26 | convolution fusion | flops 2818572288 | bytes 17629184 | tf_op jit(solution)/shard_map/dot_general | solution.py:51
  65.7 0.0 copy-done.2
  65.7 7.2 %fusion.16 = f32[192,1792]{1,0:T(8,128)S(1)} fusion(bf16[192,4096]{1,0:T(8,128)(2,1)S(1)} %copy-done.2, bf16[4096,1792]{1,0:T(8,128)(2,1)} %param.11), kind=kOutput, calls=%fused_computation.25 | convolution fusion | flops 2818572288 | bytes 17629184 | tf_op jit(solution)/shard_map/dot_general | solution.py:50
  72.9 1.9 pad_maximum_fusion
  74.8 0.0 copy-start.6
  74.8 0.0 copy-start.4
  74.8 0.0 copy-start.5
  74.8 0.0 copy-start.1
  74.8 0.0 all-reduce.3.cloned.1.call-update
  74.9 0.6 copy-done.6
  75.5 0.6 dynamic-slice
  76.7 0.0 copy-done.4
  76.7 0.0 copy-done.5
  76.7 0.1 select_reduce_fusion
  76.8 0.2 dynamic-update-slice
  77.0 10.4 %all-reduce = s32[192]{0:T(256)S(1)} all-reduce(s32[192]{0:T(256)S(1)} %dynamic-update-slice), channel_id=1, replica_groups=mesh['groups'=2,'pool'=8,'tensor'=2] {'pool'}, use_global_device_ids=true, to_apply=%add | all-reduce | flops 192 | bytes 1536
  87.5 0.1 fusion.13
  87.6 43.4 %all-gather.5.cloned.1.call-done = bf16[8,4096,64]{1,2,0:T(8,128)(2,1)} async-done(((bf16[1,4096,64]{1,2,0:T(8,128)(2,1)}), bf16[8,4096,64]{1,2,0:T(8,128)(2,1)}) %all-gather.5.cloned.1.call-update) | async-done | bytes 4194320 | tf_op jit(solution)/shard_map/all_gather | solution.py:44
  131.0 0.0 copy-done.1
  131.0 3.9 %fusion.2 = f32[24,8,64]{2,0,1:T(8,128)S(1)} fusion(bf16[8,4096,64]{1,2,0:T(8,128)(2,1)} %all-gather.5.cloned.1.call-done, bf16[24,4096]{1,0:T(8,128)(2,1)S(1)} %copy-done.1), kind=kOutput, calls=%fused_computation.7 | convolution fusion | flops 100663296 | bytes 4440064 | tf_op jit(solution)/shard_map/rd,sdk->rsk/dot_general | solution.py:41
  134.9 0.2 fusion.6
  135.1 3.3 %psum.15 = bf16[24,64]{1,0:T(8,128)(2,1)S(1)} all-reduce(f32[24,64]{1,0:T(8,128)S(1)} %bitcast.26), channel_id=1, replica_groups=mesh['groups'=2,'pool'=8,'tensor'=2] {'tensor'}, use_global_device_ids=true, to_apply=%region_2.3 | all-reduce | flops 1536 | bytes 9216 | tf_op jit(solution)/shard_map/psum | solution.py:48
  138.4 30.7 %all_gather.15 = bf16[192,64]{1,0:T(8,128)(2,1)S(1)} all-gather(bf16[24,64]{1,0:T(8,128)(2,1)S(1)} %psum.15), channel_id=1, replica_groups=mesh['groups'=2,'pool'=8,'tensor'=2] {'pool'}, dimensions={0}, use_global_device_ids=true | all-gather | bytes 27648 | tf_op jit(solution)/shard_map/all_gather | solution.py:53
  169.1 0.1 fusion.15
  169.2 0.1 copy.14
  169.2 0.1 copy.13
  169.3 0.0 copy-done
  169.3 0.0 copy-start.3
  169.4 0.4 convolution_bitcast_fusion
  169.7 0.8 copy-done.3
  170.5 1.5 convolution_bitcast_fusion.1
  172.0 0.0 all-reduce.3.cloned.1.call-done
  172.0 2.5 %fusion = f32[192,3584]{1,0:T(8,128)S(1)} fusion(f32[192,3584]{1,0:T(8,128)} %all-reduce.3.cloned.1.call-done, f32[192,1792]{1,0:T(8,128)S(1)} %convolution_bitcast_fusion, f32[192,1792]{1,0:T(8,128)} %convolution_bitcast_fusion.1), kind=kLoop, calls=%fused_computation.2 | loop fusion | flops 2064384 | bytes 8257536 | tf_op jit(solution)/shard_map/add | solution.py:57
  174.6 0.4 fusion.1
  175.0 15.1 %all_to_all.19 = bf16[8,24,1792]{2,1,0:T(8,128)(2,1)S(1)} all-to-all(bf16[8,24,1792]{2,1,0:T(8,128)(2,1)S(1)} %bitcast.24), channel_id=1, replica_groups=mesh['groups'=2,'pool'=8,'tensor'=2] {'pool'}, dimensions={0} | all-to-all | bytes 1376256 | tf_op jit(solution)/shard_map/all_to_all | solution.py:63
  190.1 0.9 copy.19
  (2 shorter events, 0.0 us)
Async XLA Ops:
  6.5 162.8 %copy-start = (bf16[8,32,1792]{2,1,0:T(8,128)(2,1)S(1)}, bf16[8,32,1792]{2,1,0:T(8,128)(2,1)}, u32[]{:S(2)}) copy-start(bf16[8,32,1792]{2,1,0:T(8,128)(2,1)} %param.15) | copy-start | bytes 2752516
  6.5 49.9 %all-gather.3.cloned.1.call-start = ((), (), s32[]{:S(2)}) async-start(), calls=%async_computation.1 | async-start | bytes 1769472 | tf_op jit(solution)/shard_map/all_gather | solution.py:49
  7.3 123.7 %all-gather.5.cloned.1.call-start = ((), (), s32[]{:S(2)}) async-start(), calls=%async_computation.3 | async-start | bytes 4718592 | tf_op jit(solution)/shard_map/all_gather | solution.py:44
  8.0 164.0 %all-reduce.3.cloned.1.call-start = ((), (), s32[]{:S(2)}) async-start(), calls=%async_computation.2 | async-start | bytes 5505024 | tf_op jit(solution)/shard_map/psum | solution.py:56
  56.5 9.2 %copy-start.2 = (bf16[192,4096]{1,0:T(8,128)(2,1)S(1)}, bf16[192,4096]{1,0:T(8,128)(2,1)}, u32[]{:S(2)}) copy-start(bf16[192,4096]{1,0:T(8,128)(2,1)} %all-gather.3.cloned.1.call-done) | copy-start | bytes 4718596
  74.8 0.7 copy-start.6
  74.8 1.9 copy-start.4
  74.8 1.9 copy-start.5
  74.8 56.1 %copy-start.1 = (bf16[24,4096]{1,0:T(8,128)(2,1)S(1)}, bf16[24,4096]{1,0:T(8,128)(2,1)}, u32[]{:S(2)}) copy-start(bf16[24,4096]{1,0:T(8,128)(2,1)} %param.8) | copy-start | bytes 589828
  169.3 1.2 copy-start.3
Sparse Core Ops, SparseCore 0:
  9.5 46.8 all-gather.2
  58.6 72.3 all-gather.4
  133.3 20.6 all-reduce.2
where the time goes:
time: 198 us
  waiting for transfers between devices  93.2 us (47%)
  blocking collectives  59.5 us (30%)
  matrix products  22.4 us (11%)
  between operations  13.9 us (7%)
  other arithmetic  5.02 us (3%)
  local copies, waits for them, and re-layouts  3.37 us (2%)
    all_gather x1, waiting for transfers between devices, body(): piece = lax.all_gather(hidden, 'pool', axis=0, tiled=True)  48.4 us
    all_gather x1, waiting for transfers between devices, body(): lax.all_gather(shrink, 'pool', axis=0, tiled=True)  43.4 us
    all_gather x1, blocking collectives, body(): reduced_rows_gathered = lax.all_gather(shrunk, 'pool', axis=0, tiled=True)  30.7 us
    all_to_all x1, blocking collectives, body(): lax.all_to_all(activated, 'pool', split_axis=0, concat_axis=1, tiled=True)  15.1 us
    unnamed x1, blocking collectives  10.4 us
    dot_general x1, matrix products, body(): up_part = jnp.dot(piece, up_weight, preferred_element_type=jnp.float32)  9.23 us
    dot_general x1, matrix products, body(): gate_part = jnp.dot(piece, gate_weight, preferred_element_type=jnp.float32)  7.2 us
  transfers between devices with their start and end apart: 3, of which 2 were waited for; matrix products, arithmetic and copies ran while one was open for 13% of the time, Pallas kernels for 0%

commit v1 on v0

--- a/solution.py
+++ b/solution.py
@@ -1,9 +1,472 @@
+import functools
+
 import jax
 import jax.numpy as jnp
 from jax import lax
+from jax.experimental import pallas as pl
+from jax.experimental.pallas import tpu as pltpu
 from jax.sharding import PartitionSpec as P
 
 adapter_scale_factor = 0.5
+LANES = 128
+BLOCK = 256
+LAG = 3
+MESH = pl.DeviceIdType.MESH
+
+
+def iota(shape, axis):
+    return lax.broadcasted_iota(jnp.int32, shape, axis)
+
+
+def fused_kernel(
+    pool,
+    ids_ref,
+    table_ref,
+    hidden_ref,
+    gate_hbm,
+    up_hbm,
+    shrink_hbm,
+    gate_expander_hbm,
+    up_expander_hbm,
+    out_ref,
+    gathered,
+    rows_in,
+    gate_w,
+    up_w,
+    shrink_w,
+    gate_expander,
+    up_expander,
+    partial,
+    partner_partial,
+    shrunk_partial,
+    shrunk_partner,
+    slot_own,
+    slot_parts,
+    gate_in,
+    up_in,
+    acted,
+    land,
+    local_sem,
+    gather_send,
+    gather_recv,
+    shrunk_sem,
+    slot_send,
+    slot_recv,
+    partial_send,
+    partial_recv,
+    act_send,
+    act_recv,
+    share_send,
+    share_recv,
+    out_sem,
+):
+    me = lax.axis_index("pool")
+    core = lax.axis_index("tensor")
+    other = 1 - core
+    z, y = me // 2, me % 2
+    depth = pool // 2
+    half_pool = pool // 2
+    own_rows, width = hidden_ref.shape
+    rows = pool * own_rows
+    half = rows // 2
+    rank2 = shrink_w.shape[1]
+    rank = rank2 // 2
+    steps = partial.shape[0]
+    stacked = gate_expander.shape[0]
+    here = core == me // half_pool
+
+    def local(i, src, dst):
+        return pltpu.make_async_copy(src, dst, local_sem.at[i])
+
+    loads = [
+        local(0, shrink_hbm, shrink_w),
+        local(1, gate_hbm, gate_w),
+        local(2, up_hbm, up_w),
+        local(3, gate_expander_hbm, gate_expander),
+        local(4, up_expander_hbm, up_expander),
+    ]
+    for load in loads:
+        load.start()
+
+    adapters = table_ref.shape[1]
+    id_hot = ids_ref[...] == iota((own_rows, adapters), 1)
+    slot = jnp.sum(jnp.where(id_hot, table_ref[...], 0), axis=1, keepdims=True)
+    hot = jnp.where(slot == iota((own_rows, LANES), 1), 1.0, 0.0).astype(jnp.bfloat16)
+    gathered[me, :, :width] = hidden_ref[...]
+    gathered[me, :, width:] = hot
+
+    barrier = pltpu.get_barrier_semaphore()
+    for step in range(1, pool):
+        pl.semaphore_signal(
+            barrier, inc=1, device_id={"pool": lax.rem(me + step, pool)}, device_id_type=MESH
+        )
+    pl.semaphore_signal(barrier, inc=1, device_id={"tensor": other}, device_id_type=MESH)
+    pl.semaphore_wait(barrier, pool)
+
+    def gather_copy(block, way, target):
+        return pltpu.make_async_remote_copy(
+            src_ref=gathered.at[block],
+            dst_ref=gathered.at[block],
+            send_sem=gather_send.at[way, block],
+            recv_sem=gather_recv.at[block],
+            device_id={"pool": target},
+            device_id_type=MESH,
+        )
+
+    def block_of(level):
+        return level * 2 + y
+
+    def to_side(level):
+        return gather_copy(block_of(level), 0, z * 2 + (1 - y))
+
+    def to_above(level):
+        return gather_copy(block_of(level), 1, (z + 1) * 2 + y)
+
+    def to_below(level):
+        return gather_copy(block_of(level), 2, (z - 1) * 2 + y)
+
+    @pl.when(z < depth - 1)
+    def _():
+        to_above(z).start()
+
+    @pl.when(z > 0)
+    def _():
+        to_below(z).start()
+
+    to_side(z).start()
+
+    def arrived(block):
+        gather_copy(block, 0, me).wait_recv()
+
+    for distance in range(1, depth):
+
+        @pl.when(z - distance >= 0)
+        def _():
+            level = z - distance
+            arrived(block_of(level))
+
+            @pl.when(z < depth - 1)
+            def _():
+                to_above(level).start()
+
+            to_side(level).start()
+
+        @pl.when(z + distance < depth)
+        def _():
+            level = z + distance
+            arrived(block_of(level))
+
+            @pl.when(z > 0)
+            def _():
+                to_below(level).start()
+
+            to_side(level).start()
+
+    for level in range(depth):
+        arrived(level * 2 + (1 - y))
+
+    for pair in range(pool // 2):
+        both = gathered[2 * pair : 2 * pair + 2].astype(jnp.float32)
+        rows_in[2 * pair * own_rows : (2 * pair + 2) * own_rows, :] = both.reshape(
+            2 * own_rows, width + LANES
+        ).astype(jnp.bfloat16)
+
+    loads[0].wait()
+    shrunk_partial[...] = jnp.dot(
+        rows_in[:, :width], shrink_w[...], preferred_element_type=jnp.float32
+    )
+    mine = pl.ds(pl.multiple_of(core * half, 16), half)
+    theirs = pl.ds(pl.multiple_of(other * half, 16), half)
+    shrunk_copy = pltpu.make_async_remote_copy(
+        src_ref=shrunk_partial.at[theirs],
+        dst_ref=shrunk_partner,
+        send_sem=shrunk_sem.at[0],
+        recv_sem=shrunk_sem.at[1],
+        device_id={"tensor": other},
+        device_id_type=MESH,
+    )
+    shrunk_copy.start()
+    for load in loads[1:]:
+        load.wait()
+
+    def slot_copy(step):
+        target = lax.rem(me + step, pool)
+        return pltpu.make_async_remote_copy(
+            src_ref=slot_own,
+            dst_ref=slot_parts.at[step],
+            send_sem=slot_send.at[step],
+            recv_sem=slot_recv.at[step],
+            device_id={"pool": target},
+            device_id_type=MESH,
+        )
+
+    def share_shrunk():
+        shrunk_copy.wait_recv()
+        mask = jnp.sum(
+            jnp.where(
+                iota((half, LANES), 1) == me, rows_in[mine, width:].astype(jnp.float32), 0.0
+            ),
+            axis=1,
+            keepdims=True,
+        )
+        total = (shrunk_partial[mine, :] + shrunk_partner[...]).astype(jnp.bfloat16)
+        slot_own[...] = jnp.where(mask > 0.5, total.astype(jnp.float32), 0.0).astype(
+            jnp.bfloat16
+        )
+        for step in range(1, pool):
+            slot_copy(step).start()
+
+    def spread_shrunk():
+        total = slot_own[...].astype(jnp.float32)
+        for step in range(1, pool):
+            slot_copy(step).wait_recv()
+            total = total + slot_parts[step].astype(jnp.float32)
+        shrunk = total.astype(jnp.bfloat16)
+        spread = jnp.where(
+            iota((LANES, stacked), 1) // rank == iota((LANES, stacked), 0), 1.0, 0.0
+        ).astype(jnp.bfloat16)
+        hot_in = jnp.dot(rows_in[mine, width:], spread, preferred_element_type=jnp.float32)
+        for offset, ref in ((0, gate_in), (rank, up_in)):
+            repeat = jnp.where(
+                iota((rank2, stacked), 1) % rank + offset == iota((rank2, stacked), 0), 1.0, 0.0
+            ).astype(jnp.bfloat16)
+            value = jnp.dot(shrunk, repeat, preferred_element_type=jnp.float32)
+            ref[...] = (value * hot_in).astype(jnp.bfloat16)
+
+    def partial_copy(c):
+        return pltpu.make_async_remote_copy(
+            src_ref=partial.at[c, :, theirs, :],
+            dst_ref=partner_partial.at[c],
+            send_sem=partial_send.at[c],
+            recv_sem=partial_recv.at[c],
+            device_id={"tensor": other},
+            device_id_type=MESH,
+        )
+
+    def act_copy(c, j):
+        target = core * half_pool + j
+        return pltpu.make_async_remote_copy(
+            src_ref=acted.at[c, j],
+            dst_ref=land.at[c, me],
+            send_sem=act_send.at[c, j],
+            recv_sem=act_recv.at[c, me],
+            device_id={"pool": target},
+            device_id_type=MESH,
+        )
+
+    def columns_of(c):
+        return pl.ds(pl.multiple_of(c * BLOCK, BLOCK), BLOCK)
+
+    def project(c):
+        columns = columns_of(c)
+        for k, weight in enumerate((gate_w, up_w)):
+            partial[c, k] = jnp.dot(
+                rows_in[:, :width], weight[:, columns], preferred_element_type=jnp.float32
+            )
+        partial_copy(c).start()
+
+    def activate(c):
+        columns = columns_of(c)
+        partial_copy(c).wait_recv()
+        pre = []
+        for k, (left, expander) in enumerate(((gate_in, gate_expander), (up_in, up_expander))):
+            change = jnp.dot(
+                left[...], expander[:, columns], preferred_element_type=jnp.float32
+            )
+            pre.append(
+                partial[c, k, mine, :] + partner_partial[c, k] + adapter_scale_factor * change
+            )
+        gate, up = pre
+        value = gate / (1.0 + jnp.exp(-gate)) * up
+        value = value.reshape(half_pool, own_rows, BLOCK).astype(jnp.bfloat16)
+        acted[c] = value
+        for j in range(half_pool):
+            is_own = core * half_pool + j == me
+
+            @pl.when(jnp.logical_not(is_own))
+            def _():
+                act_copy(c, j).start()
+
+            @pl.when(is_own)
+            def _():
+                land[c, me] = acted[c, j]
+
+    def step_body(c, carry):
+        project(c)
+
+        @pl.when(c == 0)
+        def _():
+            share_shrunk()
+
+        @pl.when(c == LAG)
+        def _():
+            spread_shrunk()
+
+        @pl.when(c >= LAG)
+        def _():
+            activate(c - LAG)
+
+        return carry
+
+    lax.fori_loop(0, steps, step_body, 0)
+
+    def late_body(c, carry):
+        activate(c)
+        return carry
+
+    lax.fori_loop(steps - LAG, steps, late_body, 0)
+
+    def share_copy(c):
+        return pltpu.make_async_remote_copy(
+            src_ref=land.at[c],
+            dst_ref=land.at[c],
+            send_sem=share_send.at[c],
+            recv_sem=share_recv.at[c],
+            device_id={"tensor": other},
+            device_id_type=MESH,
+        )
+
+    def out_copy(c):
+        return pltpu.make_async_copy(land.at[c], out_ref.at[c], out_sem.at[c])
+
+    @pl.when(here)
+    def _():
+        def receive(c, carry):
+            for step in range(1, pool):
+                source = lax.rem(me + step, pool)
+                pltpu.make_async_remote_copy(
+                    src_ref=acted.at[c, 0],
+                    dst_ref=land.at[c, source],
+                    send_sem=act_send.at[c, 0],
+                    recv_sem=act_recv.at[c, source],
+                    device_id={"pool": source},
+                    device_id_type=MESH,
+                ).wait_recv()
+            share_copy(c).start()
+            out_copy(c).start()
+            return carry
+
+        lax.fori_loop(0, steps, receive, 0)
+
+    @pl.when(jnp.logical_not(here))
+    def _():
+        def receive(c, carry):
+            share_copy(c).wait_recv()
+            out_copy(c).start()
+            return carry
+
+        lax.fori_loop(0, steps, receive, 0)
+
+    def finish(c, carry):
+        partial_copy(c).wait_send()
+        for j in range(half_pool):
+
+            @pl.when(core * half_pool + j != me)
+            def _():
+                act_copy(c, j).wait_send()
+
+        @pl.when(here)
+        def _():
+            share_copy(c).wait_send()
+
+        out_copy(c).wait()
+        return carry
+
+    lax.fori_loop(0, steps, finish, 0)
+    shrunk_copy.wait_send()
+    for step in range(1, pool):
+        slot_copy(step).wait_send()
+    for level in range(depth):
+        to_side(level).wait_send()
+
+        @pl.when(jnp.logical_and(level <= z, z < depth - 1))
+        def _():
+            to_above(level).wait_send()
+
+        @pl.when(jnp.logical_and(level >= z, z > 0))
+        def _():
+            to_below(level).wait_send()
+
+
+def fused_body(
+    pool,
+    hidden,
+    adapter_ids,
+    page_table,
+    gate_weight,
+    up_weight,
+    shrink,
+    gate_expander_matrices,
+    up_expander_matrices,
+):
+    own_rows, width = hidden.shape
+    columns = gate_weight.shape[1]
+    rank2 = shrink.shape[2]
+    steps = columns // BLOCK
+    rows = pool * own_rows
+    half = rows // 2
+    half_pool = pool // 2
+    stacked = gate_expander_matrices.shape[0] * gate_expander_matrices.shape[1]
+    bf16, f32 = jnp.bfloat16, jnp.float32
+    dma = pltpu.SemaphoreType.DMA
+    vmem = pl.BlockSpec(memory_space=pltpu.VMEM)
+    anywhere = pl.BlockSpec(memory_space=pl.ANY)
+    result = pl.pallas_call(
+        functools.partial(fused_kernel, pool),
+        out_shape=jax.ShapeDtypeStruct((steps, pool, own_rows, BLOCK), bf16),
+        in_specs=[vmem] * 3 + [anywhere] * 5,
+        out_specs=anywhere,
+        scratch_shapes=[
+            pltpu.VMEM((pool, own_rows, width + LANES), bf16),
+            pltpu.VMEM((rows, width + LANES), bf16),
+            pltpu.VMEM((width, columns), bf16),
+            pltpu.VMEM((width, columns), bf16),
+            pltpu.VMEM((width, rank2), bf16),
+            pltpu.VMEM((stacked, columns), bf16),
+            pltpu.VMEM((stacked, columns), bf16),
+            pltpu.VMEM((steps, 2, rows, BLOCK), f32),
+            pltpu.VMEM((steps, 2, half, BLOCK), f32),
+            pltpu.VMEM((rows, rank2), f32),
+            pltpu.VMEM((half, rank2), f32),
+            pltpu.VMEM((half, rank2), bf16),
+            pltpu.VMEM((pool, half, rank2), bf16),
+            pltpu.VMEM((half, stacked), bf16),
+            pltpu.VMEM((half, stacked), bf16),
+            pltpu.VMEM((steps, half_pool, own_rows, BLOCK), bf16),
+            pltpu.VMEM((steps, pool, own_rows, BLOCK), bf16),
+            dma((5,)),
+            dma((3, pool)),
+            dma((pool,)),
+            dma((2,)),
+            dma((pool,)),
+            dma((pool,)),
+            dma((steps,)),
+            dma((steps,)),
+            dma((steps, half_pool)),
+            dma((steps, pool)),
+            dma((steps,)),
+            dma((steps,)),
+            dma((steps,)),
+        ],
+        compiler_params=pltpu.CompilerParams(
+            collective_id=0, has_side_effects=True, vmem_limit_bytes=56 * 1024 * 1024
+        ),
+        cost_estimate=pl.CostEstimate(
+            flops=4 * rows * width * columns,
+            bytes_accessed=4 * width * columns,
+            transcendentals=half * columns,
+        ),
+    )(
+        adapter_ids,
+        page_table.reshape(1, -1),
+        hidden,
+        gate_weight,
+        up_weight,
+        shrink.reshape(width, rank2),
+        gate_expander_matrices.reshape(stacked, columns),
+        up_expander_matrices.reshape(stacked, columns),
+    )
+    return result.transpose(2, 1, 0, 3).reshape(own_rows, pool * columns)
 
 
 def expansion_products(shrunk_part, hot_part, gate_expander_matrices, up_expander_matrices):
@@ -63,6 +526,20 @@
     return lax.all_to_all(activated, "pool", split_axis=0, concat_axis=1, tiled=True)
 
 
+def chosen_body(pool, *args):
+    hidden, _, page_table, gate_weight, _, shrink = args[:6]
+    fits = (
+        pool % 4 == 0
+        and page_table.shape[0] == pool
+        and shrink.shape[0] == 1
+        and pool <= LANES
+        and gate_weight.shape[1] % BLOCK == 0
+        and gate_weight.shape[1] // BLOCK > LAG
+        and hidden.shape[0] % 8 == 0
+    )
+    return fused_body(pool, *args) if fits else body(*args)
+
+
 def solution(mesh):
     in_specs = (
         P(("groups", "pool"), "tensor"),
@@ -75,4 +552,10 @@
         P(None, None, "pool"),
     )
     out_specs = P(("groups", "pool"), None)
-    return jax.shard_map(body, mesh=mesh, in_specs=in_specs, out_specs=out_specs, check_vma=False)
+    return jax.shard_map(
+        functools.partial(chosen_body, mesh.shape["pool"]),
+        mesh=mesh,
+        in_specs=in_specs,
+        out_specs=out_specs,
+        check_vma=False,
+    )

time: 198 us -> 56.5 us (0.29)
  waiting for transfers between devices: 93.2 us -> 0 us
  blocking collectives: 59.5 us -> 0 us
  Pallas kernels: 0 us -> 48.9 us
  matrix products: 22.4 us -> 0 us
  between operations: 13.9 us -> 0.01 us
  other arithmetic: 5.02 us -> 0 us
  local copies, waits for them, and re-layouts: 3.37 us -> 6.8 us
    all_gather x2 -> x0, waiting for transfers between devices: 91.8 us -> none  [the longest x1 48.4 us: body(): piece = lax.all_gather(hidden, 'pool', axis=0, tiled=True)]
    pallas_call x0 -> x1, Pallas kernels: none -> 48.9 us  [fused_body(): pl.pallas_call(functools.partial(fused_kernel, pool), out_shape=jax.Shape...]
    all_gather x1 -> x0, blocking collectives: 30.7 us -> none  [body(): reduced_rows_gathered = lax.all_gather(shrunk, 'pool', axis=0, tiled=True)]
    dot_general x6 -> x0, matrix products: 22.4 us -> none  [the longest x1 9.23 us: body(): up_part = jnp.dot(piece, up_weight, preferred_element_type=jnp.float32)]
    all_to_all x1 -> x0, blocking collectives: 15.1 us -> none  [body(): lax.all_to_all(activated, 'pool', split_axis=0, concat_axis=1, tiled=True)]
    unnamed x1 -> x0, blocking collectives: 10.4 us -> none
    psum x1 -> x0, blocking collectives: 3.31 us -> none  [body(): shrunk = lax.psum(partial_value, 'tensor').astype(jnp.bfloat16)]
    add x1 -> x0, other arithmetic: 2.54 us -> none  [body(): combined_sum + adapter_scale_factor * expansion_products(reduced_rows_gat...]
  transfers between devices with their start and end apart: 3 -> 0, of which waited for: 2 -> 0; matrix products, arithmetic and copies ran while one was open for 13% -> 0% of each run, Pallas kernels for 0% -> 0%
where the time goes in v1:
time: 56.5 us; the launch traced here: 55.7 us
  Pallas kernels  48.9 us (87%)
  local copies, waits for them, and re-layouts  6.8 us (12%)
    pallas_call x1, Pallas kernels, fused_body(): pl.pallas_call(functools.partial(fused_kernel, pool), out_shape=jax.Shape...  48.9 us
    unnamed x2, local copies, waits for them, and re-layouts  3.71 us
    reshape x1, local copies, waits for them, and re-layouts, fused_body(): return result.transpose(2, 1, 0, 3).reshape(own_rows, pool * columns)  1.6 us
    transpose x1, local copies, waits for them, and re-layouts, fused_body(): return result.transpose(2, 1, 0, 3).reshape(own_rows, pool * columns)  1.49 us

profile of v1, /device:TPU:0, one launch (start us, length us, event | category | flops | bytes accessed | tf_op | source)
XLA Modules:
  0.0 55.7 jit_solution(9216516457478641590)
XLA Ops:
  0.0 1.3 %copy.12.ids_ref = s32[24,1]{1,0:T(8,128)} copy(s32[24,1]{0,1:T(1,128)} %param.9) | data formatting | bytes 192 | tf_op args[1]
  1.3 2.4 %copy.11 = bf16[1,4096,64]{2,1,0:T(8,128)(2,1)} copy(bf16[1,4096,64]{1,2,0:T(8,128)(2,1)} %param.13) | data formatting | bytes 1048576 | tf_op args[5]
  3.7 48.9 %shard_map.82 = bf16[7,8,24,256]{3,2,1,0:T(8,128)(2,1)} custom-call(s32[24,1]{1,0:T(8,128)} %copy.12.ids_ref, s32[1,8]{1,0:T(1,128)} %bitcast.9, bf16[24,4096]{1,0:T(8,128)(2,1)} %hidden_ref.1, bf16[4096,1792]{1,0:T(8,128)(2,1)} %gate_hbm.1, bf16[4096,1792]{1,0:T(8,128)(2,1)} %up_hbm.1, bf16[4096,64]{1,0:T(8,128)(2,1)} %bitcast.5, ...), custom_call_target="tpu_custom_call" | custom-call | flops 5637144576 | bytes 29360128 | tf_op jit(solution)/shard_map/pallas_call | solution.py:414
  52.6 1.5 %copy.13 = bf16[24,8,7,256]{3,2,1,0:T(8,128)(2,1)S(1)} copy(bf16[24,8,7,256]{3,0,1,2:T(8,128)(2,1)} %bitcast.6) | data formatting | bytes 1376256 | tf_op jit(solution)/shard_map/transpose | solution.py:469
  54.1 1.6 %reshape.19 = bf16[24,14336]{1,0:T(8,128)(2,1)} reshape(bf16[24,8,7,256]{3,2,1,0:T(8,128)(2,1)S(1)} %copy.13) | data formatting | bytes 1376256 | tf_op jit(solution)/shard_map/reshape | solution.py:469

commit v2 on v1

--- a/solution.py
+++ b/solution.py
@@ -16,6 +16,12 @@
 
 def iota(shape, axis):
     return lax.broadcasted_iota(jnp.int32, shape, axis)
+
+
+def dot_transposed(left, right):
+    return lax.dot_general(
+        left, right, (((1,), (1,)), ((), ())), preferred_element_type=jnp.float32
+    )
 
 
 def fused_kernel(
@@ -58,7 +64,6 @@
     act_recv,
     share_send,
     share_recv,
-    out_sem,
 ):
     me = lax.axis_index("pool")
     core = lax.axis_index("tensor")
@@ -69,7 +74,7 @@
     own_rows, width = hidden_ref.shape
     rows = pool * own_rows
     half = rows // 2
-    rank2 = shrink_w.shape[1]
+    rank2 = shrink_w.shape[0]
     rank = rank2 // 2
     steps = partial.shape[0]
     stacked = gate_expander.shape[0]
@@ -88,10 +93,15 @@
     for load in loads:
         load.start()
 
-    adapters = table_ref.shape[1]
-    id_hot = ids_ref[...] == iota((own_rows, adapters), 1)
-    slot = jnp.sum(jnp.where(id_hot, table_ref[...], 0), axis=1, keepdims=True)
-    hot = jnp.where(slot == iota((own_rows, LANES), 1), 1.0, 0.0).astype(jnp.bfloat16)
+    ids = ids_ref[...]
+    slot = jnp.zeros_like(ids)
+    for adapter in range(pool):
+        slot = jnp.where(ids == adapter, table_ref[adapter], slot)
+    hot_columns = jnp.where(slot == iota((LANES, own_rows), 0), 1.0, 0.0).astype(jnp.bfloat16)
+    unit = jnp.where(
+        iota((own_rows, own_rows), 0) == iota((own_rows, own_rows), 1), 1.0, 0.0
+    ).astype(jnp.bfloat16)
+    hot = dot_transposed(unit, hot_columns).astype(jnp.bfloat16)
     gathered[me, :, :width] = hidden_ref[...]
     gathered[me, :, width:] = hot
 
@@ -172,9 +182,7 @@
         ).astype(jnp.bfloat16)
 
     loads[0].wait()
-    shrunk_partial[...] = jnp.dot(
-        rows_in[:, :width], shrink_w[...], preferred_element_type=jnp.float32
-    )
+    shrunk_partial[...] = dot_transposed(rows_in[:, :width], shrink_w[...])
     mine = pl.ds(pl.multiple_of(core * half, 16), half)
     theirs = pl.ds(pl.multiple_of(other * half, 16), half)
     shrunk_copy = pltpu.make_async_remote_copy(
@@ -326,8 +334,10 @@
             device_id_type=MESH,
         )
 
-    def out_copy(c):
-        return pltpu.make_async_copy(land.at[c], out_ref.at[c], out_sem.at[c])
+    def place(c):
+        for source in range(pool):
+            column = pl.multiple_of((source * steps + c) * BLOCK, BLOCK)
+            out_ref[:, pl.ds(column, BLOCK)] = land[c, source]
 
     @pl.when(here)
     def _():
@@ -343,7 +353,7 @@
                     device_id_type=MESH,
                 ).wait_recv()
             share_copy(c).start()
-            out_copy(c).start()
+            place(c)
             return carry
 
         lax.fori_loop(0, steps, receive, 0)
@@ -352,7 +362,7 @@
     def _():
         def receive(c, carry):
             share_copy(c).wait_recv()
-            out_copy(c).start()
+            place(c)
             return carry
 
         lax.fori_loop(0, steps, receive, 0)
@@ -369,7 +379,6 @@
         def _():
             share_copy(c).wait_send()
 
-        out_copy(c).wait()
         return carry
 
     lax.fori_loop(0, steps, finish, 0)
@@ -413,15 +422,15 @@
     anywhere = pl.BlockSpec(memory_space=pl.ANY)
     result = pl.pallas_call(
         functools.partial(fused_kernel, pool),
-        out_shape=jax.ShapeDtypeStruct((steps, pool, own_rows, BLOCK), bf16),
-        in_specs=[vmem] * 3 + [anywhere] * 5,
-        out_specs=anywhere,
+        out_shape=jax.ShapeDtypeStruct((own_rows, pool * columns), bf16),
+        in_specs=[vmem, pl.BlockSpec(memory_space=pltpu.SMEM), vmem] + [anywhere] * 5,
+        out_specs=vmem,
         scratch_shapes=[
             pltpu.VMEM((pool, own_rows, width + LANES), bf16),
             pltpu.VMEM((rows, width + LANES), bf16),
             pltpu.VMEM((width, columns), bf16),
             pltpu.VMEM((width, columns), bf16),
-            pltpu.VMEM((width, rank2), bf16),
+            pltpu.VMEM((rank2, width), bf16),
             pltpu.VMEM((stacked, columns), bf16),
             pltpu.VMEM((stacked, columns), bf16),
             pltpu.VMEM((steps, 2, rows, BLOCK), f32),
@@ -446,7 +455,6 @@
             dma((steps, pool)),
             dma((steps,)),
             dma((steps,)),
-            dma((steps,)),
         ],
         compiler_params=pltpu.CompilerParams(
             collective_id=0, has_side_effects=True, vmem_limit_bytes=56 * 1024 * 1024
@@ -457,16 +465,16 @@
             transcendentals=half * columns,
         ),
     )(
-        adapter_ids,
-        page_table.reshape(1, -1),
+        adapter_ids.reshape(1, own_rows),
+        page_table,
         hidden,
         gate_weight,
         up_weight,
-        shrink.reshape(width, rank2),
+        shrink.reshape(width, rank2).T,
         gate_expander_matrices.reshape(stacked, columns),
         up_expander_matrices.reshape(stacked, columns),
     )
-    return result.transpose(2, 1, 0, 3).reshape(own_rows, pool * columns)
+    return result
 
 
 def expansion_products(shrunk_part, hot_part, gate_expander_matrices, up_expander_matrices):

time: 56.5 us -> 51.9 us (0.919); the launches traced: 55.7 us -> 51.7 us
  local copies, waits for them, and re-layouts: 6.8 us -> 1.99 us
  Pallas kernels: 48.9 us -> 49.7 us
    unnamed x2 -> x1, local copies, waits for them, and re-layouts: 3.71 us -> 1.99 us
    reshape x1 -> x0, local copies, waits for them, and re-layouts: 1.6 us -> none  [fused_body(): return result.transpose(2, 1, 0, 3).reshape(own_rows, pool * columns)]
    transpose x1 -> x0, local copies, waits for them, and re-layouts: 1.49 us -> none  [fused_body(): return result.transpose(2, 1, 0, 3).reshape(own_rows, pool * columns)]
    pallas_call x1, Pallas kernels: 48.9 us -> 49.7 us  [fused_body(): pl.pallas_call(functools.partial(fused_kernel, pool), out_shape=jax.Shape...]
where the time goes in v2:
time: 51.9 us; the launch traced here: 51.7 us
  Pallas kernels  49.7 us (96%)
  local copies, waits for them, and re-layouts  1.99 us (4%)
    pallas_call x1, Pallas kernels, fused_body(): pl.pallas_call(functools.partial(fused_kernel, pool), out_shape=jax.Shape...  49.7 us
    unnamed x1, local copies, waits for them, and re-layouts  1.99 us

profile of v2, /device:TPU:0, one launch (start us, length us, event | category | flops | bytes accessed | tf_op | source)
XLA Modules:
  0.0 51.7 jit_solution(1360058764300586124)
XLA Ops:
  0.0 49.7 %shard_map.82 = bf16[24,14336]{1,0:T(8,128)(2,1)} custom-call(s32[1,24]{1,0:T(1,128)} %bitcast.9, s32[8]{0:T(128)} %table_ref.1, bf16[24,4096]{1,0:T(8,128)(2,1)} %hidden_ref.1, bf16[4096,1792]{1,0:T(8,128)(2,1)} %gate_hbm.1, bf16[4096,1792]{1,0:T(8,128)(2,1)} %up_hbm.1, bf16[64,4096]{1,0:T(8,128)(2,1)} %bitcast.8, bf16[256,1792]{1,0:T(8,128)(2,1)} %bitcast.6, ...), custom_call_target="tpu_custom_call" | custom-call | flops 5637144576 | bytes 29360128 | tf_op jit(solution)/shard_map/pallas_call | solution.py:423
  49.7 2.0 %copy.10 = bf16[24,14336]{1,0:T(8,128)(2,1)} copy(bf16[24,14336]{1,0:T(8,128)(2,1)} %shard_map.82) | data formatting | bytes 1376256

commit v3 on v2

--- a/solution.py
+++ b/solution.py
@@ -10,6 +10,7 @@
 adapter_scale_factor = 0.5
 LANES = 128
 BLOCK = 256
+PIECES = 3
 LAG = 3
 MESH = pl.DeviceIdType.MESH
 
@@ -113,12 +114,14 @@
     pl.semaphore_signal(barrier, inc=1, device_id={"tensor": other}, device_id_type=MESH)
     pl.semaphore_wait(barrier, pool)
 
-    def gather_copy(block, way, target):
+    def gather_copy(block, way, target, q):
+        wide = gathered.shape[2] // PIECES
+        piece = gathered.at[block, :, pl.ds(q * wide, wide)]
         return pltpu.make_async_remote_copy(
-            src_ref=gathered.at[block],
-            dst_ref=gathered.at[block],
-            send_sem=gather_send.at[way, block],
-            recv_sem=gather_recv.at[block],
+            src_ref=piece,
+            dst_ref=piece,
+            send_sem=gather_send.at[way, q, block],
+            recv_sem=gather_recv.at[q, block],
             device_id={"pool": target},
             device_id_type=MESH,
         )
@@ -126,58 +129,81 @@
     def block_of(level):
         return level * 2 + y
 
-    def to_side(level):
-        return gather_copy(block_of(level), 0, z * 2 + (1 - y))
-
-    def to_above(level):
-        return gather_copy(block_of(level), 1, (z + 1) * 2 + y)
-
-    def to_below(level):
-        return gather_copy(block_of(level), 2, (z - 1) * 2 + y)
-
-    @pl.when(z < depth - 1)
-    def _():
-        to_above(z).start()
-
-    @pl.when(z > 0)
-    def _():
-        to_below(z).start()
-
-    to_side(z).start()
-
-    def arrived(block):
-        gather_copy(block, 0, me).wait_recv()
+    def to_side(level, q):
+        return gather_copy(block_of(level), 0, z * 2 + (1 - y), q)
+
+    def to_above(level, q):
+        return gather_copy(block_of(level), 1, (z + 1) * 2 + y, q)
+
+    def to_below(level, q):
+        return gather_copy(block_of(level), 2, (z - 1) * 2 + y, q)
+
+    near = z + 1 - 2 * (z % 2)
+    last = PIECES - 1
+
+    def across(level, q, act):
+        if q < last:
+            act(to_side(level, q))
+        else:
+
+            @pl.when(level != near)
+            def _():
+                act(to_side(level, q))
+
+    def to_near():
+        return gather_copy(z * 2 + (1 - y), 3, near * 2 + y, last)
+
+    def arrived(block, q):
+        gather_copy(block, 0, me, q).wait_recv()
+
+    for q in range(PIECES):
+
+        @pl.when(z < depth - 1)
+        def _():
+            to_above(z, q).start()
+
+        @pl.when(z > 0)
+        def _():
+            to_below(z, q).start()
+
+        to_side(z, q).start()
 
     for distance in range(1, depth):
-
-        @pl.when(z - distance >= 0)
-        def _():
-            level = z - distance
-            arrived(block_of(level))
-
-            @pl.when(z < depth - 1)
-            def _():
-                to_above(level).start()
-
-            to_side(level).start()
-
-        @pl.when(z + distance < depth)
-        def _():
-            level = z + distance
-            arrived(block_of(level))
-
-            @pl.when(z > 0)
-            def _():
-                to_below(level).start()
-
-            to_side(level).start()
-
-    for level in range(depth):
-        arrived(level * 2 + (1 - y))
-
-    for pair in range(pool // 2):
-        both = gathered[2 * pair : 2 * pair + 2].astype(jnp.float32)
-        rows_in[2 * pair * own_rows : (2 * pair + 2) * own_rows, :] = both.reshape(
+        for q in range(PIECES):
+
+            @pl.when(z - distance >= 0)
+            def _():
+                level = z - distance
+                arrived(block_of(level), q)
+
+                @pl.when(z < depth - 1)
+                def _():
+                    to_above(level, q).start()
+
+                across(level, q, lambda copy: copy.start())
+
+            @pl.when(z + distance < depth)
+            def _():
+                level = z + distance
+                arrived(block_of(level), q)
+
+                @pl.when(z > 0)
+                def _():
+                    to_below(level, q).start()
+
+                across(level, q, lambda copy: copy.start())
+
+    arrived(z * 2 + (1 - y), last)
+    to_near().start()
+
+    for order in range(depth):
+        level = 2 * ((z // 2 + order // 2) % (depth // 2)) + (z + order) % 2
+        for q in range(PIECES):
+            if order > 0 or q < last:
+                arrived(level * 2 + (1 - y), q)
+        both = gathered[pl.ds(level * 2, 2)].astype(jnp.float32)
+        start = pl.multiple_of(level * (2 * own_rows), 16)
+        rows_in[pl.ds(start, 2 * own_rows), :] = both.reshape(
             2 * own_rows, width + LANES
         ).astype(jnp.bfloat16)
 
@@ -386,15 +412,18 @@
     for step in range(1, pool):
         slot_copy(step).wait_send()
     for level in range(depth):
-        to_side(level).wait_send()
-
-        @pl.when(jnp.logical_and(level <= z, z < depth - 1))
-        def _():
-            to_above(level).wait_send()
-
-        @pl.when(jnp.logical_and(level >= z, z > 0))
-        def _():
-            to_below(level).wait_send()
+        for q in range(PIECES):
+            across(level, q, lambda copy: copy.wait_send())
+
+            @pl.when(jnp.logical_and(level <= z, z < depth - 1))
+            def _():
+                to_above(level, q).wait_send()
+
+            @pl.when(jnp.logical_and(level >= z, z > 0))
+            def _():
+                to_below(level, q).wait_send()
+
+    to_near().wait_send()
 
 
 def fused_body(
@@ -444,8 +473,8 @@
             pltpu.VMEM((steps, half_pool, own_rows, BLOCK), bf16),
             pltpu.VMEM((steps, pool, own_rows, BLOCK), bf16),
             dma((5,)),
-            dma((3, pool)),
-            dma((pool,)),
+            dma((4, PIECES, pool)),
+            dma((PIECES, pool)),
             dma((2,)),
             dma((pool,)),
             dma((pool,)),
@@ -544,6 +573,7 @@
         and gate_weight.shape[1] % BLOCK == 0
         and gate_weight.shape[1] // BLOCK > LAG
         and hidden.shape[0] % 8 == 0
+        and (hidden.shape[1] + LANES) % (PIECES * LANES) == 0
     )
     return fused_body(pool, *args) if fits else body(*args)
 

time: 51.9 us -> 51.2 us (0.987)
  Pallas kernels: 49.7 us -> 49 us
    pallas_call x1, Pallas kernels: 49.7 us -> 49 us  [fused_body(): pl.pallas_call(functools.partial(fused_kernel, pool), out_shape=jax.Shape...]
where the time goes in v3:
time: 51.2 us; the launch traced here: 51 us
  Pallas kernels  49 us (96%)
  local copies, waits for them, and re-layouts  1.99 us (4%)
    pallas_call x1, Pallas kernels, fused_body(): pl.pallas_call(functools.partial(fused_kernel, pool), out_shape=jax.Shape...  49 us
    unnamed x1, local copies, waits for them, and re-layouts  1.99 us

profile of v3, /device:TPU:0, one launch (start us, length us, event | category | flops | bytes accessed | tf_op | source)
XLA Modules:
  0.0 51.0 jit_solution(3005601749430559492)
XLA Ops:
  0.0 49.0 %shard_map.82 = bf16[24,14336]{1,0:T(8,128)(2,1)} custom-call(s32[1,24]{1,0:T(1,128)} %bitcast.9, s32[8]{0:T(128)} %table_ref.1, bf16[24,4096]{1,0:T(8,128)(2,1)} %hidden_ref.1, bf16[4096,1792]{1,0:T(8,128)(2,1)} %gate_hbm.1, bf16[4096,1792]{1,0:T(8,128)(2,1)} %up_hbm.1, bf16[64,4096]{1,0:T(8,128)(2,1)} %bitcast.8, bf16[256,1792]{1,0:T(8,128)(2,1)} %bitcast.6, ...), custom_call_target="tpu_custom_call" | custom-call | flops 5637144576 | bytes 29360128 | tf_op jit(solution)/shard_map/pallas_call | solution.py:452
  49.0 2.0 %copy.10 = bf16[24,14336]{1,0:T(8,128)(2,1)} copy(bf16[24,14336]{1,0:T(8,128)(2,1)} %shard_map.82) | data formatting | bytes 1376256

commit v4 on v3

--- a/solution.py
+++ b/solution.py
@@ -11,7 +11,7 @@
 LANES = 128
 BLOCK = 256
 PIECES = 3
-LAG = 3
+LAG = 2
 MESH = pl.DeviceIdType.MESH
 
 
@@ -168,6 +168,16 @@
 
         to_side(z, q).start()
 
+    def take(order):
+        level = 2 * ((z // 2 + order // 2) % (depth // 2)) + (z + order) % 2
+        for q in range(PIECES):
+            arrived(level * 2 + (1 - y), q)
+        both = gathered[pl.ds(level * 2, 2)].astype(jnp.float32)
+        both = both.reshape(2 * own_rows, width + LANES).astype(jnp.bfloat16)
+        taken = pl.ds(pl.multiple_of(level * (2 * own_rows), 16), 2 * own_rows)
+        rows_in[taken, :] = both
+        shrunk_partial[taken, :] = dot_transposed(both[:, :width], shrink_w[...])
+
     for distance in range(1, depth):
         for q in range(PIECES):
 
@@ -193,22 +203,14 @@
 
                 across(level, q, lambda copy: copy.start())
 
-    arrived(z * 2 + (1 - y), last)
+        if distance == 1:
+            loads[0].wait()
+            take(0)
+
     to_near().start()
-
-    for order in range(depth):
-        level = 2 * ((z // 2 + order // 2) % (depth // 2)) + (z + order) % 2
-        for q in range(PIECES):
-            if order > 0 or q < last:
-                arrived(level * 2 + (1 - y), q)
-        both = gathered[pl.ds(level * 2, 2)].astype(jnp.float32)
-        start = pl.multiple_of(level * (2 * own_rows), 16)
-        rows_in[pl.ds(start, 2 * own_rows), :] = both.reshape(
-            2 * own_rows, width + LANES
-        ).astype(jnp.bfloat16)
-
-    loads[0].wait()
-    shrunk_partial[...] = dot_transposed(rows_in[:, :width], shrink_w[...])
+    for order in range(1, depth):
+        take(order)
+
     mine = pl.ds(pl.multiple_of(core * half, 16), half)
     theirs = pl.ds(pl.multiple_of(other * half, 16), half)
     shrunk_copy = pltpu.make_async_remote_copy(

time: 51.2 us -> 51.7 us (level)
  no operation moved by 1% of the time
where the time goes in v4:
time: 51.7 us; the launch traced here: 51.5 us
  Pallas kernels  49.5 us (96%)
  local copies, waits for them, and re-layouts  1.99 us (4%)
    pallas_call x1, Pallas kernels, fused_body(): pl.pallas_call(functools.partial(fused_kernel, pool), out_shape=jax.Shape...  49.5 us
    unnamed x1, local copies, waits for them, and re-layouts  1.99 us

profile of v4, /device:TPU:0, one launch (start us, length us, event | category | flops | bytes accessed | tf_op | source)
XLA Modules:
  0.0 51.5 jit_solution(11845497106351823275)
XLA Ops:
  0.0 49.5 %shard_map.82 = bf16[24,14336]{1,0:T(8,128)(2,1)} custom-call(s32[1,24]{1,0:T(1,128)} %bitcast.9, s32[8]{0:T(128)} %table_ref.1, bf16[24,4096]{1,0:T(8,128)(2,1)} %hidden_ref.1, bf16[4096,1792]{1,0:T(8,128)(2,1)} %gate_hbm.1, bf16[4096,1792]{1,0:T(8,128)(2,1)} %up_hbm.1, bf16[64,4096]{1,0:T(8,128)(2,1)} %bitcast.8, bf16[256,1792]{1,0:T(8,128)(2,1)} %bitcast.6, ...), custom_call_target="tpu_custom_call" | custom-call | flops 5637144576 | bytes 29360128 | tf_op jit(solution)/shard_map/pallas_call | solution.py:454
  49.5 2.0 %copy.10 = bf16[24,14336]{1,0:T(8,128)(2,1)} copy(bf16[24,14336]{1,0:T(8,128)(2,1)} %shard_map.82) | data formatting | bytes 1376256

commit v5 on v4

--- a/solution.py
+++ b/solution.py
@@ -11,7 +11,7 @@
 LANES = 128
 BLOCK = 256
 PIECES = 3
-LAG = 2
+LAG = 4
 MESH = pl.DeviceIdType.MESH
 
 

time: 51.7 us -> 51.3 us (level)
  no operation moved by 1% of the time
where the time goes in v5:
time: 51.3 us; the launch traced here: 51.2 us
  Pallas kernels  49.2 us (96%)
  local copies, waits for them, and re-layouts  1.99 us (4%)
    pallas_call x1, Pallas kernels, fused_body(): pl.pallas_call(functools.partial(fused_kernel, pool), out_shape=jax.Shape...  49.2 us
    unnamed x1, local copies, waits for them, and re-layouts  1.99 us

profile of v5, /device:TPU:0, one launch (start us, length us, event | category | flops | bytes accessed | tf_op | source)
XLA Modules:
  0.0 51.2 jit_solution(18307301628185928618)
XLA Ops:
  0.0 49.2 %shard_map.82 = bf16[24,14336]{1,0:T(8,128)(2,1)} custom-call(s32[1,24]{1,0:T(1,128)} %bitcast.9, s32[8]{0:T(128)} %table_ref.1, bf16[24,4096]{1,0:T(8,128)(2,1)} %hidden_ref.1, bf16[4096,1792]{1,0:T(8,128)(2,1)} %gate_hbm.1, bf16[4096,1792]{1,0:T(8,128)(2,1)} %up_hbm.1, bf16[64,4096]{1,0:T(8,128)(2,1)} %bitcast.8, bf16[256,1792]{1,0:T(8,128)(2,1)} %bitcast.6, ...), custom_call_target="tpu_custom_call" | custom-call | flops 5637144576 | bytes 29360128 | tf_op jit(solution)/shard_map/pallas_call | solution.py:454
  49.2 2.0 %copy.10 = bf16[24,14336]{1,0:T(8,128)(2,1)} copy(bf16[24,14336]{1,0:T(8,128)(2,1)} %shard_map.82) | data formatting | bytes 1376256

commit v6 on v5

--- a/solution.py
+++ b/solution.py
@@ -81,6 +81,13 @@
     stacked = gate_expander.shape[0]
     here = core == me // half_pool
 
+    barrier = pltpu.get_barrier_semaphore()
+    for step in range(1, pool):
+        pl.semaphore_signal(
+            barrier, inc=1, device_id={"pool": lax.rem(me + step, pool)}, device_id_type=MESH
+        )
+    pl.semaphore_signal(barrier, inc=1, device_id={"tensor": other}, device_id_type=MESH)
+
     def local(i, src, dst):
         return pltpu.make_async_copy(src, dst, local_sem.at[i])
 
@@ -106,12 +113,6 @@
     gathered[me, :, :width] = hidden_ref[...]
     gathered[me, :, width:] = hot
 
-    barrier = pltpu.get_barrier_semaphore()
-    for step in range(1, pool):
-        pl.semaphore_signal(
-            barrier, inc=1, device_id={"pool": lax.rem(me + step, pool)}, device_id_type=MESH
-        )
-    pl.semaphore_signal(barrier, inc=1, device_id={"tensor": other}, device_id_type=MESH)
     pl.semaphore_wait(barrier, pool)
 
     def gather_copy(block, way, target, q):

time: 51.3 us -> 51.2 us (level)
  no operation moved by 1% of the time
where the time goes in v6:
time: 51.2 us; the launch traced here: 51.1 us
  Pallas kernels  49.1 us (96%)
  local copies, waits for them, and re-layouts  1.99 us (4%)
    pallas_call x1, Pallas kernels, fused_body(): pl.pallas_call(functools.partial(fused_kernel, pool), out_shape=jax.Shape...  49.1 us
    unnamed x1, local copies, waits for them, and re-layouts  1.99 us

profile of v6, /device:TPU:0, one launch (start us, length us, event | category | flops | bytes accessed | tf_op | source)
XLA Modules:
  0.0 51.1 jit_solution(892887405431022717)
XLA Ops:
  0.0 49.1 %shard_map.82 = bf16[24,14336]{1,0:T(8,128)(2,1)} custom-call(s32[1,24]{1,0:T(1,128)} %bitcast.9, s32[8]{0:T(128)} %table_ref.1, bf16[24,4096]{1,0:T(8,128)(2,1)} %hidden_ref.1, bf16[4096,1792]{1,0:T(8,128)(2,1)} %gate_hbm.1, bf16[4096,1792]{1,0:T(8,128)(2,1)} %up_hbm.1, bf16[64,4096]{1,0:T(8,128)(2,1)} %bitcast.8, bf16[256,1792]{1,0:T(8,128)(2,1)} %bitcast.6, ...), custom_call_target="tpu_custom_call" | custom-call | flops 5637144576 | bytes 29360128 | tf_op jit(solution)/shard_map/pallas_call | solution.py:455
  49.1 2.0 %copy.10 = bf16[24,14336]{1,0:T(8,128)(2,1)} copy(bf16[24,14336]{1,0:T(8,128)(2,1)} %shard_map.82) | data formatting | bytes 1376256
